TPU v7x, 32 devices: a whole 2x2x4 slice. The times are simulated.
32 devices in a mesh: grp: 2 (over y), leaf: 4 (over z), limb: 2 (over x), coef: 2 (over core).
Axes of the slice: x: 2, y: 2, z: 4, core: 2. Of those that a mesh axis runs over, the one named last changes fastest.
Arguments:
- root_keys: bfloat16 [8, 1, 2, 12, 256, 128], P(('grp', 'leaf'), None, None, 'limb', 'coef'), parts along dimension 0, may hold values from -6 to 6
- switch_main: bfloat16 [8, 2, 4, 2, 12, 256, 128], P(('grp', 'leaf'), None, None, None, 'limb', 'coef'), parts along dimension 0, may hold values from -3 to 3
- switch_special: bfloat16 [8, 2, 4, 2, 4, 256, 128], P(('grp', 'leaf'), None, None, None, 'limb', 'coef'), parts along dimension 0, may hold values from -3 to 3
- basis_up: bfloat16 [4, 16, 3], replicated, may hold values from -3.5 to 3.5
- basis_down: bfloat16 [12, 4], P('limb'), may hold values from -3 to 3
- special_inverse: float32 [12], P('limb'), may hold values from 0.5 to 2
- parent_table: int32 [2, 8], P(None, 'grp'), parts along dimension 1, may hold values from 0 to 3, as said below
- owner_table: int32 [8], P('grp'), parts along dimension 0, may hold values from 0 to 3, as said below
Outputs:
- delivered: bfloat16 [8, 3, 1, 2, 12, 256, 128], P(('grp', 'leaf'), None, None, None, 'limb', 'coef'), parts along dimension 0
There are 2 independent parts, one for each index of `grp`. A program takes and returns all parts, laid end to end along the dimension named above; an argument that names none is the same for every part. Nothing has to cross between parts.
Inputs may be any that keep to these rules, and one draw needn't show every extreme that they name: parent_table[l, j] = (j + e) mod 4 with e from -2 to 2; in every row e = 2 for some j and e = -2 for another j. `owner_table`: each value is taken by at most 3 entries, and by exactly 3 entries for some value.
All inputs are finite; a program needn't handle non-finite values.
Results may differ from a plain program's by a relative error of at most 0.025.
Values may be sent and summed in bfloat16 or wider, within the bound.
A program may use at most 64 MiB of HBM per device.

v0:
```python
import functools
import math

import jax
import jax.numpy as jnp
import ml_dtypes
import numpy as np
from jax import lax
from jax.experimental import pallas as pl
from jax.experimental.pallas import tpu as pltpu
from jax.sharding import PartitionSpec as P

MESH = pl.DeviceIdType.MESH
CHUNK = 3


def cosine_table(length):
    frequency = np.arange(length).astype(np.float32)[:, None]
    sample = np.arange(length).astype(np.float32)[None, :]
    weight = np.where(
        frequency == 0, np.sqrt(np.float32(1.0 / length)), np.sqrt(np.float32(2.0 / length))
    )
    angle = np.float32(math.pi) * (np.float32(2.0) * sample + np.float32(1.0)) * frequency
    angle = angle / np.float32(2.0 * length)
    return (weight * np.cos(angle)).astype(ml_dtypes.bfloat16)


def twist_table(limbs, n1, n2):
    product = (
        (2 * np.arange(limbs) + 1)[:, None, None]
        * np.arange(n2)[None, :, None]
        * np.arange(n1)[None, None, :]
        % n2
    )
    return 1.0 + 0.5 * np.cos(2.0 * math.pi * product / n2)


def dot(a, b):
    return jnp.dot(a, b, preferred_element_type=jnp.float32)


def pick(n, index, load):
    if n <= 8:
        value = load(0)
        for j in range(1, n):
            value = jnp.where(index == j, load(j), value)
        return value
    return lax.fori_loop(
        1, n, lambda j, value: jnp.where(index == j, load(j), value), load(0)
    )


def repeat(low, high, body):
    if high - low <= 3:
        for i in range(low, high):
            body(i)
    else:
        lax.fori_loop(low, high, lambda i, c: (body(i), c)[1], 0)


def kernel(
    cfg,
    parent_ref,
    owner_ref,
    up_ref,
    down_ref,
    inv_ref,
    c1_ref,
    c1t_ref,
    d_ref,
    root_ref,
    main_hbm,
    special_hbm,
    twist_hbm,
    recip_hbm,
    out_ref,
    main_key,
    special_key,
    twist,
    recip,
    z_buf,
    x_gather,
    b_gather,
    f_gather,
    x_buf,
    z2_buf,
    x2_buf,
    s_main,
    s_special,
    b_add,
    load_sem,
    route_send,
    route_recv,
    z_sem,
    x_send,
    x_recv,
    z2_sem,
    x2_send,
    x2_recv,
):
    n, nl, lm, ls, lq, lp, digits, levels, cap, half = cfg
    width = CHUNK
    chunks = lm // width
    me = lax.axis_index("leaf")
    limb = lax.axis_index("limb")
    coef = lax.axis_index("coef")
    other = 1 - coef

    loads = []
    for l in range(levels):
        loads.append(pltpu.make_async_copy(main_hbm.at[0, l], main_key.at[l], load_sem.at[l]))
        loads.append(
            pltpu.make_async_copy(special_hbm.at[0, l], special_key.at[l], load_sem.at[levels + l])
        )
    rows = pl.ds(pl.multiple_of(coef * half, half), half)
    tables = []
    for k, (src, dst) in enumerate(((recip_hbm, recip), (twist_hbm, twist))):
        tables.append(
            pltpu.make_async_copy(
                src.at[pl.ds(limb * lm, lm), rows], dst.at[pl.ds(0, lm)], load_sem.at[2 * levels + 2 * k]
            )
        )
        tables.append(
            pltpu.make_async_copy(
                src.at[pl.ds(lq + limb * ls, ls), rows],
                dst.at[pl.ds(lm, ls)],
                load_sem.at[2 * levels + 2 * k + 1],
            )
        )
    for copy in tables + loads:
        copy.start()

    barrier = pltpu.get_barrier_semaphore()

    @pl.when(me > 0)
    def _():
        pl.semaphore_signal(barrier, inc=1, device_id={"leaf": me - 1}, device_id_type=MESH)

    @pl.when(me < n - 1)
    def _():
        pl.semaphore_signal(barrier, inc=1, device_id={"leaf": me + 1}, device_id_type=MESH)

    pl.semaphore_signal(barrier, inc=1, device_id={"coef": other}, device_id_type=MESH)
    for k in range(1, nl):
        pl.semaphore_signal(
            barrier, inc=1, device_id={"limb": lax.rem(limb + k, nl)}, device_id_type=MESH
        )
    neighbours = jnp.where(me > 0, 1, 0) + jnp.where(me < n - 1, 1, 0)
    pl.semaphore_wait(barrier, nl + neighbours)

    def hop(unit, piece, slot, c, way):
        target = me + 1 if way == 0 else me - 1
        return pltpu.make_async_remote_copy(
            src_ref=piece(slot, c),
            dst_ref=piece(slot, c),
            send_sem=route_send.at[unit, way, slot, c],
            recv_sem=route_recv.at[unit, slot, c],
            device_id={"leaf": target},
            device_id_type=MESH,
        )

    def route_start(unit, piece, c):
        @pl.when(me < n - 1)
        def _():
            hop(unit, piece, me, c, 0).start()

        @pl.when(me > 0)
        def _():
            hop(unit, piece, me, c, 1).start()

    def route_step(unit, piece, s, c):
        @pl.when(me >= s)
        def _():
            hop(unit, piece, me - s, c, 0).wait_recv()

            @pl.when(me < n - 1)
            def _():
                hop(unit, piece, me - s, c, 0).start()

        @pl.when(me + s <= n - 1)
        def _():
            hop(unit, piece, me + s, c, 1).wait_recv()

            @pl.when(me > 0)
            def _():
                hop(unit, piece, me + s, c, 1).start()

    def route_steps(unit, piece, low, high):
        def one(s):
            for c in range(chunks):
                route_step(unit, piece, s, c)

        repeat(low, high, one)

    def route_end(unit, piece):
        def one(slot):
            for c in range(chunks):

                @pl.when((slot <= me) & (me < n - 1))
                def _():
                    hop(unit, piece, slot, c, 0).wait_send()

                @pl.when((slot >= me) & (me > 0))
                def _():
                    hop(unit, piece, slot, c, 1).wait_send()

        repeat(0, n, one)

    def part(c):
        return pl.ds(c * width, width)

    def piece_of(buf, *lead):
        return lambda slot, c: buf.at[(*lead, slot, part(c))]

    c1 = c1_ref[...]
    c1t = c1t_ref[...]
    d_own = d_ref[rows, :]

    def z_copy(buf, sem, l, c, where):
        return pltpu.make_async_remote_copy(
            src_ref=buf.at[l, coef, where],
            dst_ref=buf.at[l, coef, where],
            send_sem=sem.at[l, 0, c],
            recv_sem=sem.at[l, 1, c],
            device_id={"coef": other},
            device_id_type=MESH,
        )

    def mixed(buf, l, t):
        own = buf[l, coef, t].astype(jnp.float32)
        return own + dot(d_own[:, :half], buf[l, 0, t]) + dot(d_own[:, half:], buf[l, 1, t])

    def x_copy(l, c, k):
        return pltpu.make_async_remote_copy(
            src_ref=x_buf.at[l, limb, part(c)],
            dst_ref=x_buf.at[l, limb, part(c)],
            send_sem=x_send.at[l, c, k - 1],
            recv_sem=x_recv.at[l, c, k - 1],
            device_id={"limb": lax.rem(limb + k, nl)},
            device_id_type=MESH,
        )

    def x2_copy(l, k):
        return pltpu.make_async_remote_copy(
            src_ref=x2_buf.at[l, limb],
            dst_ref=x2_buf.at[l, limb],
            send_sem=x2_send.at[l, k - 1],
            recv_sem=x2_recv.at[l, k - 1],
            device_id={"limb": lax.rem(limb + k, nl)},
            device_id_type=MESH,
        )

    def switched(l, t_global, t_twist, key_of):
        sums = [None, None]
        w = twist[t_twist]
        for d in range(digits):
            total = None
            for s in range(CHUNK):
                at = d * CHUNK + s
                term = x_buf[l, at // lm, at % lm].astype(jnp.float32)
                term = term * up_ref[(d * (lq + lp) + t_global) * CHUNK + s]
                total = term if total is None else total + term
            hat = dot((total * w).astype(jnp.bfloat16), c1t)
            for i in range(2):
                add = hat * key_of(d, i).astype(jnp.float32)
                sums[i] = add if sums[i] is None else sums[i] + add
        return sums

    def corrected(l, i, q):
        total = None
        for p in range(lp):
            term = x2_buf[l, p // ls, i * ls + p % ls].astype(jnp.float32) * down_ref[q * lp + p]
            total = term if total is None else total + term
        hat = dot((total * twist[q]).astype(jnp.bfloat16), c1t)
        return (s_main[i, q] - hat) * inv_ref[q]

    b_gather[0, me] = root_ref[0]
    tables[0].wait()
    tables[1].wait()

    def send_z(l, t, value):
        z_buf[l, coef, t] = (dot(value, c1) * recip[t]).astype(jnp.bfloat16)

    for c in range(chunks):
        for t in range(c * width, (c + 1) * width):
            send_z(0, t, root_ref[1, t])
        z_copy(z_buf, z_sem, 0, c, part(c)).start()
    tables[2].wait()
    tables[3].wait()

    for l in range(levels):
        parent = parent_ref[l * n + me]
        xp = piece_of(x_gather, l)
        bp = piece_of(b_gather, l)
        ux, ub = 2 * l, 2 * l + 1
        for c in range(chunks):
            z_copy(z_buf, z_sem, l, c, part(c)).wait_recv()
            for t in range(c * width, (c + 1) * width):
                x_gather[l, me, t] = mixed(z_buf, l, t).astype(jnp.bfloat16)
            route_start(ux, xp, c)
        if l > 0:
            route_steps(ub - 2, piece_of(b_gather, l - 1), 2, n)
            before = parent_ref[(l - 1) * n + me]
            for t in range(lm):
                held = pick(n, before, lambda j: b_gather[l - 1, j, t]).astype(jnp.float32)
                b_gather[l, me, t] = (held + b_add[t]).astype(jnp.bfloat16)
        route_steps(ux, xp, 1, n - 1)
        for c in range(chunks):
            route_step(ux, xp, n - 1, c)
            for t in range(c * width, (c + 1) * width):
                x_buf[l, limb, t] = pick(n, parent, lambda j: x_gather[l, j, t])
            for k in range(1, nl):
                x_copy(l, c, k).start()
            route_start(ub, bp, c)
        loads[2 * l].wait()
        loads[2 * l + 1].wait()
        for c in range(chunks):
            for k in range(1, nl):
                x_copy(l, c, k).wait_recv()

        for p in range(ls):
            sums = switched(
                l, lq + limb * ls + p, lm + p, lambda d, i: special_key[l, d, i, p]
            )
            for i in range(2):
                z = dot(sums[i].astype(jnp.bfloat16), c1) * recip[lm + p]
                z2_buf[l, coef, i * ls + p] = z.astype(jnp.bfloat16)
        everything = pl.ds(0, 2 * ls)
        z_copy(z2_buf, z2_sem, l, 0, everything).start()
        z_copy(z2_buf, z2_sem, l, 0, everything).wait_recv()
        for e in range(2 * ls):
            x2_buf[l, limb, e] = mixed(z2_buf, l, e).astype(jnp.bfloat16)
        for k in range(1, nl):
            x2_copy(l, k).start()

        def main_target(t, carry):
            sums = switched(l, limb * lm + t, t, lambda d, i: main_key[l, d, i, t])
            s_main[0, t] = sums[0]
            s_main[1, t] = sums[1]
            return carry

        lax.fori_loop(0, lm, main_target, 0)
        for k in range(1, nl):
            x2_copy(l, k).wait_recv()

        last = l == levels - 1
        for c in range(chunks):
            for t in range(c * width, (c + 1) * width):
                value = corrected(l, 1, t).astype(jnp.bfloat16)
                if last:
                    f_gather[1, me, t] = value
                else:
                    send_z(l + 1, t, value)
            if last:
                route_start(2 * levels, piece_of(f_gather, 1), c)
            else:
                z_copy(z_buf, z_sem, l + 1, c, part(c)).start()
        route_steps(ub, bp, 1, 2)

        def b_part(t, carry):
            b_add[t] = corrected(l, 0, t)
            return carry

        lax.fori_loop(0, lm, b_part, 0)

    l = levels - 1
    route_steps(2 * l + 1, piece_of(b_gather, l), 2, n)
    before = parent_ref[l * n + me]
    fa, fb = piece_of(f_gather, 1), piece_of(f_gather, 0)
    for c in range(chunks):
        for t in range(c * width, (c + 1) * width):
            held = pick(n, before, lambda j: b_gather[l, j, t]).astype(jnp.float32)
            f_gather[0, me, t] = (held + b_add[t]).astype(jnp.bfloat16)
        route_start(2 * levels + 1, fb, c)

    def both(s):
        for c in range(chunks):
            route_step(2 * levels, fa, s, c)
        for c in range(chunks):
            route_step(2 * levels + 1, fb, s, c)

    repeat(1, n, both)

    def seek(j, state):
        count, sources, found = state
        mine = (owner_ref[j] == me).astype(jnp.int32)
        hits = [mine * (count == s).astype(jnp.int32) for s in range(cap)]
        sources = tuple(src + hit * j for src, hit in zip(sources, hits))
        found = tuple(f + hit for f, hit in zip(found, hits))
        return count + mine, sources, found

    zero = jnp.int32(0)
    _, sources, found = lax.fori_loop(0, n, seek, (zero, (zero,) * cap, (zero,) * cap))
    for s in range(cap):
        for i in range(2):
            value = f_gather[i, sources[s]]
            out_ref[s, i] = jnp.where(found[s] > 0, value, jnp.zeros_like(value))

    for l in range(levels):
        route_end(2 * l, piece_of(x_gather, l))
        route_end(2 * l + 1, piece_of(b_gather, l))
        for c in range(chunks):
            z_copy(z_buf, z_sem, l, c, part(c)).wait_send()
            for k in range(1, nl):
                x_copy(l, c, k).wait_send()
        z_copy(z2_buf, z2_sem, l, 0, pl.ds(0, 2 * ls)).wait_send()
        for k in range(1, nl):
            x2_copy(l, k).wait_send()
    route_end(2 * levels, fa)
    route_end(2 * levels + 1, fb)


def per_device(
    n,
    nl,
    nc,
    root_keys,
    switch_main,
    switch_special,
    basis_up,
    basis_down,
    special_inverse,
    parent_table,
    owner_table,
):
    cap = 3
    _, levels, digits, _, lm, half, n1 = switch_main.shape
    ls = switch_special.shape[4]
    lq, lp = lm * nl, ls * nl
    n2 = half * nc
    chunks = lm // CHUNK
    c1 = cosine_table(n1)
    c2 = cosine_table(n2).astype(np.float64)
    gram = (c2 @ c2.T - np.eye(n2)).astype(np.float32).astype(ml_dtypes.bfloat16)
    table = twist_table(lq + lp, n1, n2)
    cfg = (n, nl, lm, ls, lq, lp, digits, levels, cap, half)
    bf16, f32 = jnp.bfloat16, jnp.float32
    tile = (half, n1)
    smem = pl.BlockSpec(memory_space=pltpu.SMEM)
    vmem = pl.BlockSpec(memory_space=pltpu.VMEM)
    hbm = pl.BlockSpec(memory_space=pl.ANY)
    dma = pltpu.SemaphoreType.DMA
    units = 2 * levels + 2
    out = pl.pallas_call(
        functools.partial(kernel, cfg),
        out_shape=jax.ShapeDtypeStruct((cap, 2, lm) + tile, bf16),
        in_specs=[smem] * 5 + [vmem] * 4 + [hbm] * 4,
        out_specs=vmem,
        scratch_shapes=[
            pltpu.VMEM((levels, digits, 2, lm) + tile, bf16),
            pltpu.VMEM((levels, digits, 2, ls) + tile, bf16),
            pltpu.VMEM((lm + ls,) + tile, f32),
            pltpu.VMEM((lm + ls,) + tile, f32),
            pltpu.VMEM((levels, 2, lm) + tile, bf16),
            pltpu.VMEM((levels, n, lm) + tile, bf16),
            pltpu.VMEM((levels, n, lm) + tile, bf16),
            pltpu.VMEM((2, n, lm) + tile, bf16),
            pltpu.VMEM((levels, nl, lm) + tile, bf16),
            pltpu.VMEM((levels, 2, 2 * ls) + tile, bf16),
            pltpu.VMEM((levels, nl, 2 * ls) + tile, bf16),
            pltpu.VMEM((2, lm) + tile, f32),
            pltpu.VMEM((2, ls) + tile, f32),
            pltpu.VMEM((lm,) + tile, f32),
            dma((2 * levels + 4,)),
            dma((units, 2, n, chunks)),
            dma((units, n, chunks)),
            dma((levels, 2, chunks)),
            dma((levels, chunks, nl - 1)),
            dma((levels, chunks, nl - 1)),
            dma((levels, 2, 1)),
            dma((levels, nl - 1)),
            dma((levels, nl - 1)),
        ],
        compiler_params=pltpu.CompilerParams(
            collective_id=0, has_side_effects=True, vmem_limit_bytes=56 * 1024 * 1024
        ),
        name="derive_and_deliver",
    )(
        parent_table.reshape(-1),
        owner_table,
        basis_up.astype(f32).reshape(-1),
        basis_down.astype(f32).reshape(-1),
        special_inverse,
        jnp.asarray(c1),
        jnp.asarray(np.ascontiguousarray(c1.T)),
        jnp.asarray(gram),
        root_keys.reshape((2, lm) + tile),
        switch_main,
        switch_special,
        jnp.asarray(table.astype(np.float32)),
        jnp.asarray((1.0 / table).astype(np.float32)),
    )
    return out.reshape((1, cap, 1, 2, lm) + tile)


def solution(mesh):
    sizes = [mesh.shape[axis] for axis in ("leaf", "limb", "coef")]
    return jax.shard_map(
        functools.partial(per_device, *sizes),
        mesh=mesh,
        in_specs=(
            P(("grp", "leaf"), None, None, "limb", "coef", None),
            P(("grp", "leaf"), None, None, None, "limb", "coef", None),
            P(("grp", "leaf"), None, None, None, "limb", "coef", None),
            P(),
            P("limb", None),
            P("limb"),
            P(None, "grp"),
            P("grp"),
        ),
        out_specs=P(("grp", "leaf"), None, None, None, "limb", "coef", None),
        check_vma=False,
    )
```

profile of v0, /device:TPU:0, one launch (start us, length us, event | category | flops | bytes accessed | tf_op | source)
XLA Modules:
  0.0 102.0 jit_solution(7908486616237482469)
XLA Ops:
  0.0 1.3 %reshape.19.parent_ref = s32[8]{0:T(128)} reshape(s32[2,4]{1,0:T(2,128)} %param.19) | data formatting | bytes 64 | tf_op jit(solution)/shard_map/reshape | solution.py:479
  1.3 0.8 copy.17
  2.1 0.6 reshape.29.down_ref
  2.7 0.8 copy.16
  3.5 0.7 reshape.27.up_ref
  4.2 95.3 %derive_and_deliver.1 = bf16[3,2,6,128,128]{4,3,2,1,0:T(8,128)(2,1)} custom-call(s32[8]{0:T(128)} %reshape.19.parent_ref, s32[4]{0:T(128)} %owner_ref.1, f32[192]{0:T(256)} %reshape.27.up_ref, f32[24]{0:T(128)} %reshape.29.down_ref, f32[6]{0:T(128)} %inv_ref.1, bf16[128,128]{1,0:T(8,128)(2,1)} %constant.10.clone.c1_ref, ...), custom_call_target="tpu_custom_call" | custom-call | tf_op jit(solution)/shard_map/derive_and_deliver/pallas_call | solution.py:444
  99.5 2.4 %copy.20 = bf16[1,3,1,2,6,128,128]{6,5,4,3,2,1,0:T(8,128)(2,1)} copy(bf16[1,3,1,2,6,128,128]{6,5,4,3,2,1,0:T(8,128)(2,1)} %bitcast.4) | data formatting | bytes 2359296
where the time goes:
time: 102 us
  Pallas kernels  95.3 us (93%)
  local copies, waits for them, and re-layouts  6.61 us (6%)
    pallas_call x1, Pallas kernels, per_device(): pl.pallas_call(functools.partial(kernel, cfg), out_shape=jax.ShapeDtypeSt...  95.3 us
    unnamed x1, local copies, waits for them, and re-layouts  2.41 us

commit v1 on v0

--- a/solution.py
+++ b/solution.py
@@ -51,7 +51,7 @@
 
 
 def repeat(low, high, body):
-    if high - low <= 3:
+    if high - low <= 8:
         for i in range(low, high):
             body(i)
     else:
@@ -88,8 +88,14 @@
     s_main,
     s_special,
     b_add,
+    stage,
+    up_f32,
+    down_f32,
+    up_smem,
+    down_smem,
     load_sem,
     route_send,
+    relay_send,
     route_recv,
     z_sem,
     x_send,
@@ -127,90 +133,164 @@
                 load_sem.at[2 * levels + 2 * k + 1],
             )
         )
-    for copy in tables + loads:
+    up_f32[...] = up_ref[...].astype(jnp.float32)
+    down_f32[...] = down_ref[...].astype(jnp.float32)
+    scalars = [
+        pltpu.make_async_copy(up_f32, up_smem, load_sem.at[2 * levels + 4]),
+        pltpu.make_async_copy(down_f32, down_smem, load_sem.at[2 * levels + 5]),
+    ]
+    for copy in tables + loads + scalars:
         copy.start()
 
     barrier = pltpu.get_barrier_semaphore()
 
-    @pl.when(me > 0)
-    def _():
-        pl.semaphore_signal(barrier, inc=1, device_id={"leaf": me - 1}, device_id_type=MESH)
-
-    @pl.when(me < n - 1)
-    def _():
-        pl.semaphore_signal(barrier, inc=1, device_id={"leaf": me + 1}, device_id_type=MESH)
-
+    def greet(target):
+        meets = (target > 0) & (target < n - 1) | (me > 0) & (me < n - 1)
+
+        @pl.when((target != me) & meets)
+        def _():
+            pl.semaphore_signal(barrier, inc=1, device_id={"leaf": target}, device_id_type=MESH)
+
+    repeat(0, n, greet)
     pl.semaphore_signal(barrier, inc=1, device_id={"coef": other}, device_id_type=MESH)
     for k in range(1, nl):
         pl.semaphore_signal(
             barrier, inc=1, device_id={"limb": lax.rem(limb + k, nl)}, device_id_type=MESH
         )
-    neighbours = jnp.where(me > 0, 1, 0) + jnp.where(me < n - 1, 1, 0)
-    pl.semaphore_wait(barrier, nl + neighbours)
-
-    def hop(unit, piece, slot, c, way):
-        target = me + 1 if way == 0 else me - 1
-        return pltpu.make_async_remote_copy(
-            src_ref=piece(slot, c),
-            dst_ref=piece(slot, c),
-            send_sem=route_send.at[unit, way, slot, c],
-            recv_sem=route_recv.at[unit, slot, c],
-            device_id={"leaf": target},
-            device_id_type=MESH,
-        )
-
-    def route_start(unit, piece, c):
-        @pl.when(me < n - 1)
-        def _():
-            hop(unit, piece, me, c, 0).start()
-
-        @pl.when(me > 0)
-        def _():
-            hop(unit, piece, me, c, 1).start()
-
-    def route_step(unit, piece, s, c):
-        @pl.when(me >= s)
-        def _():
-            hop(unit, piece, me - s, c, 0).wait_recv()
-
-            @pl.when(me < n - 1)
+    at_end = (me == 0) | (me == n - 1)
+    pl.semaphore_wait(barrier, nl + jnp.where(at_end, n - 2, n - 1))
+
+    ends = ((n - 2, n - 1, 0), (1, 0, 1))
+    inner = (me > 0) & (me < n - 1)
+
+    class Route:
+        def __init__(self, unit, buf, lead, width, whole):
+            self.unit, self.buf, self.lead, self.width, self.whole = unit, buf, lead, width, whole
+            self.chunks = lm // width
+
+        def piece(self, slot, c):
+            return self.buf.at[self.lead, slot, pl.ds(c * self.width, self.width)]
+
+        def hop(self, slot, c, target):
+            return pltpu.make_async_remote_copy(
+                src_ref=self.piece(slot, c),
+                dst_ref=self.piece(slot, c),
+                send_sem=route_send.at[self.unit, target, c],
+                recv_sem=route_recv.at[self.unit, slot, c],
+                device_id={"leaf": target},
+                device_id_type=MESH,
+            )
+
+        def relay(self, c, end, side, slot):
+            if self.whole:
+                source = self.piece(slot, c)
+            else:
+                source = stage.at[self.unit, side, pl.ds(c * self.width, self.width)]
+            return pltpu.make_async_remote_copy(
+                src_ref=source,
+                dst_ref=self.piece(slot, c),
+                send_sem=relay_send.at[self.unit, side, slot, c],
+                recv_sem=route_recv.at[self.unit, slot, c],
+                device_id={"leaf": end},
+                device_id_type=MESH,
+            )
+
+        def start(self, c):
+            def one(target):
+                @pl.when(target != me)
+                def _():
+                    self.hop(me, c, target).start()
+
+            if self.whole:
+                for near, end, side in ends:
+
+                    @pl.when(me == near)
+                    def _():
+                        self.relay(c, end, side, me).start()
+
+            repeat(1, n - 1, one)
+
+        def arrive(self, c, needed=None):
+            @pl.when(inner)
             def _():
-                hop(unit, piece, me - s, c, 0).start()
-
-        @pl.when(me + s <= n - 1)
-        def _():
-            hop(unit, piece, me + s, c, 1).wait_recv()
-
-            @pl.when(me > 0)
+                def one(slot):
+                    @pl.when(slot != me)
+                    def _():
+                        self.hop(slot, c, lax.rem(me + 1, n)).wait_recv()
+                        if self.whole:
+                            for near, end, side in ends:
+
+                                @pl.when((me == near) & (slot != end))
+                                def _():
+                                    self.relay(c, end, side, slot).start()
+
+                repeat(0, n, one)
+                if not self.whole:
+                    for near, end, side in ends:
+
+                        @pl.when(me == near)
+                        def _():
+                            for t in range(c * self.width, (c + 1) * self.width):
+                                stage[self.unit, side, t] = self.choose(needed[side], t)
+                            self.relay(c, end, side, me).start()
+
+        def settle(self, c):
+            for near, end, side in ends:
+
+                @pl.when(me == end)
+                def _():
+                    if self.whole:
+
+                        def one(slot):
+                            @pl.when(slot != end)
+                            def _():
+                                self.hop(slot, c, near).wait_recv()
+
+                        repeat(0, n, one)
+                    else:
+                        self.hop(near, c, near).wait_recv()
+
+        def choose(self, index, t):
+            return pick(n, index, lambda j: self.buf[self.lead, j, t])
+
+        def take(self, index, t, use):
+            @pl.when(inner)
             def _():
-                hop(unit, piece, me + s, c, 1).start()
-
-    def route_steps(unit, piece, low, high):
-        def one(s):
-            for c in range(chunks):
-                route_step(unit, piece, s, c)
-
-        repeat(low, high, one)
-
-    def route_end(unit, piece):
-        def one(slot):
-            for c in range(chunks):
-
-                @pl.when((slot <= me) & (me < n - 1))
+                use(self.choose(index, t))
+
+            for near, end, side in ends:
+
+                @pl.when(me == end)
                 def _():
-                    hop(unit, piece, slot, c, 0).wait_send()
-
-                @pl.when((slot >= me) & (me > 0))
-                def _():
-                    hop(unit, piece, slot, c, 1).wait_send()
-
-        repeat(0, n, one)
+                    own = self.buf[self.lead, end, t]
+                    use(jnp.where(index == end, own, self.buf[self.lead, near, t]))
+
+        def end(self):
+            for c in range(self.chunks):
+
+                def one(target):
+                    @pl.when(target != me)
+                    def _():
+                        self.hop(me, c, target).wait_send()
+
+                repeat(1, n - 1, one)
+                for near, end, side in ends:
+
+                    @pl.when(me == near)
+                    def _():
+                        if self.whole:
+
+                            def other_slot(slot):
+                                @pl.when(slot != end)
+                                def _():
+                                    self.relay(c, end, side, slot).wait_send()
+
+                            repeat(0, n, other_slot)
+                        else:
+                            self.relay(c, end, side, me).wait_send()
 
     def part(c):
         return pl.ds(c * width, width)
-
-    def piece_of(buf, *lead):
-        return lambda slot, c: buf.at[(*lead, slot, part(c))]
 
     c1 = c1_ref[...]
     c1t = c1t_ref[...]
@@ -232,8 +312,8 @@
 
     def x_copy(l, c, k):
         return pltpu.make_async_remote_copy(
-            src_ref=x_buf.at[l, limb, part(c)],
-            dst_ref=x_buf.at[l, limb, part(c)],
+            src_ref=x_buf.at[l, limb, c],
+            dst_ref=x_buf.at[l, limb, c],
             send_sem=x_send.at[l, c, k - 1],
             recv_sem=x_recv.at[l, c, k - 1],
             device_id={"limb": lax.rem(limb + k, nl)},
@@ -258,7 +338,7 @@
             for s in range(CHUNK):
                 at = d * CHUNK + s
                 term = x_buf[l, at // lm, at % lm].astype(jnp.float32)
-                term = term * up_ref[(d * (lq + lp) + t_global) * CHUNK + s]
+                term = term * up_smem[d, t_global, s]
                 total = term if total is None else total + term
             hat = dot((total * w).astype(jnp.bfloat16), c1t)
             for i in range(2):
@@ -269,10 +349,24 @@
     def corrected(l, i, q):
         total = None
         for p in range(lp):
-            term = x2_buf[l, p // ls, i * ls + p % ls].astype(jnp.float32) * down_ref[q * lp + p]
+            term = x2_buf[l, p // ls, i * ls + p % ls].astype(jnp.float32) * down_smem[q, p]
             total = term if total is None else total + term
         hat = dot((total * twist[q]).astype(jnp.bfloat16), c1t)
         return (s_main[i, q] - hat) * inv_ref[q]
+
+    def put(buf, where, value):
+        buf[where] = value
+
+    def finish_b(l, use):
+        way_b = ways[l][1]
+        for c in range(chunks):
+            way_b.settle(c)
+            for t in range(c * width, (c + 1) * width):
+                way_b.take(
+                    parent_ref[l, me],
+                    t,
+                    lambda held: use(t, (held.astype(jnp.float32) + b_add[t]).astype(jnp.bfloat16)),
+                )
 
     b_gather[0, me] = root_ref[0]
     tables[0].wait()
@@ -288,35 +382,39 @@
     tables[2].wait()
     tables[3].wait()
 
+    ways = [
+        (Route(2 * l, x_gather, l, 1, False), Route(2 * l + 1, b_gather, l, width, False))
+        for l in range(levels)
+    ]
+    final = [Route(2 * levels + i, f_gather, i, width, True) for i in range(2)]
+
     for l in range(levels):
-        parent = parent_ref[l * n + me]
-        xp = piece_of(x_gather, l)
-        bp = piece_of(b_gather, l)
-        ux, ub = 2 * l, 2 * l + 1
+        parent = parent_ref[l, me]
+        needed = (parent_ref[l, n - 1], parent_ref[l, 0])
+        way_x, way_b = ways[l]
         for c in range(chunks):
             z_copy(z_buf, z_sem, l, c, part(c)).wait_recv()
             for t in range(c * width, (c + 1) * width):
                 x_gather[l, me, t] = mixed(z_buf, l, t).astype(jnp.bfloat16)
-            route_start(ux, xp, c)
+                way_x.start(t)
         if l > 0:
-            route_steps(ub - 2, piece_of(b_gather, l - 1), 2, n)
-            before = parent_ref[(l - 1) * n + me]
-            for t in range(lm):
-                held = pick(n, before, lambda j: b_gather[l - 1, j, t]).astype(jnp.float32)
-                b_gather[l, me, t] = (held + b_add[t]).astype(jnp.bfloat16)
-        route_steps(ux, xp, 1, n - 1)
-        for c in range(chunks):
-            route_step(ux, xp, n - 1, c)
-            for t in range(c * width, (c + 1) * width):
-                x_buf[l, limb, t] = pick(n, parent, lambda j: x_gather[l, j, t])
+            finish_b(l - 1, lambda t, value: put(b_gather, (l, me, t), value))
+        for t in range(lm):
+            way_x.arrive(t, needed)
+            way_x.settle(t)
+            way_x.take(parent, t, lambda value: put(x_buf, (l, limb, t), value))
             for k in range(1, nl):
-                x_copy(l, c, k).start()
-            route_start(ub, bp, c)
+                x_copy(l, t, k).start()
+        for c in range(chunks):
+            way_b.start(c)
+        if l == 0:
+            for copy in scalars:
+                copy.wait()
         loads[2 * l].wait()
         loads[2 * l + 1].wait()
-        for c in range(chunks):
+        for t in range(lm):
             for k in range(1, nl):
-                x_copy(l, c, k).wait_recv()
+                x_copy(l, t, k).wait_recv()
 
         for p in range(ls):
             sums = switched(
@@ -352,34 +450,27 @@
                 else:
                     send_z(l + 1, t, value)
             if last:
-                route_start(2 * levels, piece_of(f_gather, 1), c)
+                final[1].start(c)
             else:
                 z_copy(z_buf, z_sem, l + 1, c, part(c)).start()
-        route_steps(ub, bp, 1, 2)
 
         def b_part(t, carry):
             b_add[t] = corrected(l, 0, t)
             return carry
 
         lax.fori_loop(0, lm, b_part, 0)
-
-    l = levels - 1
-    route_steps(2 * l + 1, piece_of(b_gather, l), 2, n)
-    before = parent_ref[l * n + me]
-    fa, fb = piece_of(f_gather, 1), piece_of(f_gather, 0)
+        for c in range(chunks):
+            way_b.arrive(c, needed)
+
+    finish_b(levels - 1, lambda t, value: put(f_gather, (0, me, t), value))
     for c in range(chunks):
-        for t in range(c * width, (c + 1) * width):
-            held = pick(n, before, lambda j: b_gather[l, j, t]).astype(jnp.float32)
-            f_gather[0, me, t] = (held + b_add[t]).astype(jnp.bfloat16)
-        route_start(2 * levels + 1, fb, c)
-
-    def both(s):
-        for c in range(chunks):
-            route_step(2 * levels, fa, s, c)
-        for c in range(chunks):
-            route_step(2 * levels + 1, fb, s, c)
-
-    repeat(1, n, both)
+        final[0].start(c)
+    for way in (final[1], final[0]):
+        for c in range(chunks):
+            way.arrive(c)
+    for way in (final[1], final[0]):
+        for c in range(chunks):
+            way.settle(c)
 
     def seek(j, state):
         count, sources, found = state
@@ -397,17 +488,18 @@
             out_ref[s, i] = jnp.where(found[s] > 0, value, jnp.zeros_like(value))
 
     for l in range(levels):
-        route_end(2 * l, piece_of(x_gather, l))
-        route_end(2 * l + 1, piece_of(b_gather, l))
+        for way in ways[l]:
+            way.end()
         for c in range(chunks):
             z_copy(z_buf, z_sem, l, c, part(c)).wait_send()
+        for t in range(lm):
             for k in range(1, nl):
-                x_copy(l, c, k).wait_send()
+                x_copy(l, t, k).wait_send()
         z_copy(z2_buf, z2_sem, l, 0, pl.ds(0, 2 * ls)).wait_send()
         for k in range(1, nl):
             x2_copy(l, k).wait_send()
-    route_end(2 * levels, fa)
-    route_end(2 * levels + 1, fb)
+    for way in final:
+        way.end()
 
 
 def per_device(
@@ -444,7 +536,7 @@
     out = pl.pallas_call(
         functools.partial(kernel, cfg),
         out_shape=jax.ShapeDtypeStruct((cap, 2, lm) + tile, bf16),
-        in_specs=[smem] * 5 + [vmem] * 4 + [hbm] * 4,
+        in_specs=[smem] * 2 + [vmem] * 2 + [smem] + [vmem] * 4 + [hbm] * 4,
         out_specs=vmem,
         scratch_shapes=[
             pltpu.VMEM((levels, digits, 2, lm) + tile, bf16),
@@ -461,12 +553,18 @@
             pltpu.VMEM((2, lm) + tile, f32),
             pltpu.VMEM((2, ls) + tile, f32),
             pltpu.VMEM((lm,) + tile, f32),
-            dma((2 * levels + 4,)),
-            dma((units, 2, n, chunks)),
-            dma((units, n, chunks)),
+            pltpu.VMEM((2 * levels, 2, lm) + tile, bf16),
+            pltpu.VMEM(basis_up.shape, f32),
+            pltpu.VMEM(basis_down.shape, f32),
+            pltpu.SMEM(basis_up.shape, f32),
+            pltpu.SMEM(basis_down.shape, f32),
+            dma((2 * levels + 6,)),
+            dma((units, n, lm)),
+            dma((units, 2, n, lm)),
+            dma((units, n, lm)),
             dma((levels, 2, chunks)),
-            dma((levels, chunks, nl - 1)),
-            dma((levels, chunks, nl - 1)),
+            dma((levels, lm, nl - 1)),
+            dma((levels, lm, nl - 1)),
             dma((levels, 2, 1)),
             dma((levels, nl - 1)),
             dma((levels, nl - 1)),
@@ -476,10 +574,10 @@
         ),
         name="derive_and_deliver",
     )(
-        parent_table.reshape(-1),
+        parent_table,
         owner_table,
-        basis_up.astype(f32).reshape(-1),
-        basis_down.astype(f32).reshape(-1),
+        basis_up,
+        basis_down,
         special_inverse,
         jnp.asarray(c1),
         jnp.asarray(np.ascontiguousarray(c1.T)),

time: 102 us -> 93.9 us (0.921)
  Pallas kernels: 95.3 us -> 88.5 us
  local copies, waits for them, and re-layouts: 6.61 us -> 5.14 us
    pallas_call x1, Pallas kernels: 95.3 us -> 88.5 us  [per_device(): pl.pallas_call(functools.partial(kernel, cfg), out_shape=jax.ShapeDtypeSt...]
    reshape x5 -> x0, local copies, waits for them, and re-layouts: 4.2 us -> none  [the longest x2 1.49 us: per_device(): basis_up.astype(f32).reshape(-1)]
    unnamed x1 -> x3, local copies, waits for them, and re-layouts: 2.41 us -> 5.14 us
where the time goes in v1:
time: 93.9 us; the launch traced here: 93.7 us
  Pallas kernels  88.5 us (94%)
  local copies, waits for them, and re-layouts  5.14 us (5%)
    pallas_call x1, Pallas kernels, per_device(): pl.pallas_call(functools.partial(kernel, cfg), out_shape=jax.ShapeDtypeSt...  88.5 us
    unnamed x3, local copies, waits for them, and re-layouts  5.14 us

profile of v1, /device:TPU:0, one launch (start us, length us, event | category | flops | bytes accessed | tf_op | source)
XLA Modules:
  0.0 93.7 jit_solution(2707532386267918152)
XLA Ops:
  0.0 1.3 %copy.15.down_ref = bf16[6,4]{1,0:T(8,128)(2,1)} copy(bf16[6,4]{0,1:T(4,128)(2,1)} %param.17) | data formatting | bytes 96 | tf_op args[4]
  1.3 1.4 %copy.14.up_ref = bf16[4,16,3]{2,1,0:T(8,128)(2,1)} copy(bf16[4,16,3]{1,0,2:T(4,128)(2,1)} %param.16) | data formatting | bytes 768 | tf_op args[3]
  2.7 88.5 %derive_and_deliver.1 = bf16[3,2,6,128,128]{4,3,2,1,0:T(8,128)(2,1)} custom-call(s32[2,4]{1,0:T(2,128)} %parent_ref.1, s32[4]{0:T(128)} %owner_ref.1, bf16[4,16,3]{2,1,0:T(8,128)(2,1)} %copy.14.up_ref, bf16[6,4]{1,0:T(8,128)(2,1)} %copy.15.down_ref, f32[6]{0:T(128)} %inv_ref.1, bf16[128,128]{1,0:T(8,128)(2,1)} %constant.10.clone.c1_ref, ...), custom_call_target="tpu_custom_call" | custom-call | tf_op jit(solution)/shard_map/derive_and_deliver/pallas_call | solution.py:536
  91.3 2.4 %copy.18 = bf16[1,3,1,2,6,128,128]{6,5,4,3,2,1,0:T(8,128)(2,1)} copy(bf16[1,3,1,2,6,128,128]{6,5,4,3,2,1,0:T(8,128)(2,1)} %bitcast.4) | data formatting | bytes 2359296

commit v2 on v1

--- a/solution.py
+++ b/solution.py
@@ -61,7 +61,6 @@
 def kernel(
     cfg,
     parent_ref,
-    owner_ref,
     up_ref,
     down_ref,
     inv_ref,
@@ -94,6 +93,7 @@
     up_smem,
     down_smem,
     load_sem,
+    store_sem,
     route_send,
     relay_send,
     route_recv,
@@ -331,16 +331,20 @@
         )
 
     def switched(l, t_global, t_twist, key_of):
-        sums = [None, None]
         w = twist[t_twist]
+        turned = []
         for d in range(digits):
             total = None
             for s in range(CHUNK):
                 at = d * CHUNK + s
                 term = x_buf[l, at // lm, at % lm].astype(jnp.float32)
-                term = term * up_smem[d, t_global, s]
+                term = term * up_smem[s, d, t_global]
                 total = term if total is None else total + term
-            hat = dot((total * w).astype(jnp.bfloat16), c1t)
+            turned.append((total * w).astype(jnp.bfloat16))
+        hats = dot(jnp.concatenate(turned, axis=0), c1t)
+        sums = [None, None]
+        for d in range(digits):
+            hat = hats[d * half : (d + 1) * half]
             for i in range(2):
                 add = hat * key_of(d, i).astype(jnp.float32)
                 sums[i] = add if sums[i] is None else sums[i] + add
@@ -349,7 +353,7 @@
     def corrected(l, i, q):
         total = None
         for p in range(lp):
-            term = x2_buf[l, p // ls, i * ls + p % ls].astype(jnp.float32) * down_smem[q, p]
+            term = x2_buf[l, p // ls, i * ls + p % ls].astype(jnp.float32) * down_smem[p, q]
             total = term if total is None else total + term
         hat = dot((total * twist[q]).astype(jnp.bfloat16), c1t)
         return (s_main[i, q] - hat) * inv_ref[q]
@@ -359,7 +363,15 @@
 
     def finish_b(l, use):
         way_b = ways[l][1]
-        for c in range(chunks):
+
+        def b_part(c, carry):
+            for t in range(width):
+                b_add[c * width + t] = corrected(l, 0, c * width + t)
+            return carry
+
+        lax.fori_loop(0, chunks, b_part, 0)
+        for c in range(chunks):
+            way_b.arrive(c, (parent_ref[l, n - 1], parent_ref[l, 0]))
             way_b.settle(c)
             for t in range(c * width, (c + 1) * width):
                 way_b.take(
@@ -431,13 +443,15 @@
         for k in range(1, nl):
             x2_copy(l, k).start()
 
-        def main_target(t, carry):
-            sums = switched(l, limb * lm + t, t, lambda d, i: main_key[l, d, i, t])
-            s_main[0, t] = sums[0]
-            s_main[1, t] = sums[1]
+        def main_targets(c, carry):
+            for t in range(width):
+                at = c * width + t
+                sums = switched(l, limb * lm + at, at, lambda d, i: main_key[l, d, i, at])
+                s_main[0, at] = sums[0]
+                s_main[1, at] = sums[1]
             return carry
 
-        lax.fori_loop(0, lm, main_target, 0)
+        lax.fori_loop(0, chunks, main_targets, 0)
         for k in range(1, nl):
             x2_copy(l, k).wait_recv()
 
@@ -454,38 +468,37 @@
             else:
                 z_copy(z_buf, z_sem, l + 1, c, part(c)).start()
 
-        def b_part(t, carry):
-            b_add[t] = corrected(l, 0, t)
-            return carry
-
-        lax.fori_loop(0, lm, b_part, 0)
-        for c in range(chunks):
-            way_b.arrive(c, needed)
-
     finish_b(levels - 1, lambda t, value: put(f_gather, (0, me, t), value))
     for c in range(chunks):
         final[0].start(c)
-    for way in (final[1], final[0]):
-        for c in range(chunks):
-            way.arrive(c)
-    for way in (final[1], final[0]):
-        for c in range(chunks):
-            way.settle(c)
-
-    def seek(j, state):
-        count, sources, found = state
-        mine = (owner_ref[j] == me).astype(jnp.int32)
-        hits = [mine * (count == s).astype(jnp.int32) for s in range(cap)]
-        sources = tuple(src + hit * j for src, hit in zip(sources, hits))
-        found = tuple(f + hit for f, hit in zip(found, hits))
-        return count + mine, sources, found
-
-    zero = jnp.int32(0)
-    _, sources, found = lax.fori_loop(0, n, seek, (zero, (zero,) * cap, (zero,) * cap))
-    for s in range(cap):
-        for i in range(2):
-            value = f_gather[i, sources[s]]
-            out_ref[s, i] = jnp.where(found[s] > 0, value, jnp.zeros_like(value))
+    def store(i, c):
+        def one(slot):
+            pltpu.make_async_copy(
+                final[i].piece(slot, c),
+                out_ref.at[i, slot, part(c)],
+                store_sem.at[i, slot, c],
+            ).start()
+
+        repeat(0, n, one)
+
+    for i in (1, 0):
+        for c in range(chunks):
+            final[i].arrive(c)
+    for i in (1, 0):
+        for c in range(chunks):
+            final[i].settle(c)
+            store(i, c)
+    for i in (1, 0):
+        for c in range(chunks):
+
+            def stored(slot):
+                pltpu.make_async_copy(
+                    final[i].piece(slot, c),
+                    out_ref.at[i, slot, part(c)],
+                    store_sem.at[i, slot, c],
+                ).wait()
+
+            repeat(0, n, stored)
 
     for l in range(levels):
         for way in ways[l]:
@@ -500,6 +513,38 @@
             x2_copy(l, k).wait_send()
     for way in final:
         way.end()
+
+
+def deliver(n, cap, owner_ref, keys_ref, out_ref, zeros, sem):
+    me = lax.axis_index("leaf")
+    zeros[...] = jnp.zeros_like(zeros)
+
+    def seek(j, state):
+        count, sources, found = state
+        mine = (owner_ref[j] == me).astype(jnp.int32)
+        hits = [mine * (count == s).astype(jnp.int32) for s in range(cap)]
+        sources = tuple(src + hit * j for src, hit in zip(sources, hits))
+        found = tuple(f + hit for f, hit in zip(found, hits))
+        return count + mine, sources, found
+
+    zero = jnp.int32(0)
+    _, sources, found = lax.fori_loop(0, n, seek, (zero, (zero,) * cap, (zero,) * cap))
+    for s in range(cap):
+        for i in range(2):
+
+            @pl.when(found[s] > 0)
+            def _():
+                pltpu.make_async_copy(
+                    keys_ref.at[i, sources[s]], out_ref.at[s, i], sem.at[s, i]
+                ).start()
+
+            @pl.when(found[s] == 0)
+            def _():
+                pltpu.make_async_copy(zeros, out_ref.at[s, i], sem.at[s, i]).start()
+
+    for s in range(cap):
+        for i in range(2):
+            pltpu.make_async_copy(zeros, out_ref.at[s, i], sem.at[s, i]).wait()
 
 
 def per_device(
@@ -525,6 +570,8 @@
     c2 = cosine_table(n2).astype(np.float64)
     gram = (c2 @ c2.T - np.eye(n2)).astype(np.float32).astype(ml_dtypes.bfloat16)
     table = twist_table(lq + lp, n1, n2)
+    basis_up = basis_up.transpose(2, 0, 1)
+    basis_down = basis_down.T
     cfg = (n, nl, lm, ls, lq, lp, digits, levels, cap, half)
     bf16, f32 = jnp.bfloat16, jnp.float32
     tile = (half, n1)
@@ -533,11 +580,11 @@
     hbm = pl.BlockSpec(memory_space=pl.ANY)
     dma = pltpu.SemaphoreType.DMA
     units = 2 * levels + 2
-    out = pl.pallas_call(
+    keys = pl.pallas_call(
         functools.partial(kernel, cfg),
-        out_shape=jax.ShapeDtypeStruct((cap, 2, lm) + tile, bf16),
-        in_specs=[smem] * 2 + [vmem] * 2 + [smem] + [vmem] * 4 + [hbm] * 4,
-        out_specs=vmem,
+        out_shape=jax.ShapeDtypeStruct((2, n, lm) + tile, bf16),
+        in_specs=[smem, vmem, vmem, smem] + [vmem] * 4 + [hbm] * 4,
+        out_specs=hbm,
         scratch_shapes=[
             pltpu.VMEM((levels, digits, 2, lm) + tile, bf16),
             pltpu.VMEM((levels, digits, 2, ls) + tile, bf16),
@@ -559,6 +606,7 @@
             pltpu.SMEM(basis_up.shape, f32),
             pltpu.SMEM(basis_down.shape, f32),
             dma((2 * levels + 6,)),
+            dma((2, n, chunks)),
             dma((units, n, lm)),
             dma((units, 2, n, lm)),
             dma((units, n, lm)),
@@ -575,7 +623,6 @@
         name="derive_and_deliver",
     )(
         parent_table,
-        owner_table,
         basis_up,
         basis_down,
         special_inverse,
@@ -588,6 +635,15 @@
         jnp.asarray(table.astype(np.float32)),
         jnp.asarray((1.0 / table).astype(np.float32)),
     )
+    out = pl.pallas_call(
+        functools.partial(deliver, n, cap),
+        out_shape=jax.ShapeDtypeStruct((cap, 2, lm) + tile, bf16),
+        in_specs=[smem, hbm],
+        out_specs=hbm,
+        scratch_shapes=[pltpu.VMEM((lm,) + tile, bf16), dma((cap, 2))],
+        compiler_params=pltpu.CompilerParams(vmem_limit_bytes=56 * 1024 * 1024),
+        name="deliver",
+    )(owner_table, keys)
     return out.reshape((1, cap, 1, 2, lm) + tile)
 
 

time: 93.9 us -> 121 us (1.29)
  the two profiles are of different devices: /device:TPU:0 before, /device:TPU:23 now
where the time goes in v2:
time: 121 us
  Pallas kernels  121 us (100%)
    pallas_call x1, Pallas kernels, per_device(): pl.pallas_call(functools.partial(kernel, cfg), out_shape=jax.ShapeDtypeSt...  83.7 us
    pallas_call x1, Pallas kernels, per_device(): pl.pallas_call(functools.partial(deliver, n, cap), out_shape=jax.ShapeDty...  37.6 us

profile of v2, /device:TPU:23, one launch (start us, length us, event | category | flops | bytes accessed | tf_op | source)
XLA Modules:
  0.0 121.3 jit_solution(3032550319989717048)
XLA Ops:
  0.0 83.7 %derive_and_deliver.1.keys_ref = bf16[2,4,6,128,128]{4,3,2,1,0:T(8,128)(2,1)} custom-call(s32[2,4]{1,0:T(2,128)} %parent_ref.1, bf16[3,4,16]{2,1,0:T(4,128)(2,1)} %bitcast.7, bf16[4,6]{1,0:T(4,128)(2,1)} %bitcast.8, f32[6]{0:T(128)} %inv_ref.1, bf16[128,128]{1,0:T(8,128)(2,1)} %constant.10.clone.c1_ref, bf16[128,128]{1,0:T(8,128)(2,1)} %constant.11.clone.c1t_ref, ...), custom_call_target="tpu_custom_call" | custom-call | tf_op jit(solution)/shard_map/derive_and_deliver/pallas_call | solution.py:583
  83.7 37.6 %deliver.1 = bf16[3,2,6,128,128]{4,3,2,1,0:T(8,128)(2,1)} custom-call(s32[4]{0:T(128)} %owner_ref.1, bf16[2,4,6,128,128]{4,3,2,1,0:T(8,128)(2,1)} %derive_and_deliver.1.keys_ref), custom_call_target="tpu_custom_call" | custom-call | tf_op jit(solution)/shard_map/deliver/pallas_call | solution.py:638

commit v3 on v2

--- a/solution.py
+++ b/solution.py
@@ -320,12 +320,12 @@
             device_id_type=MESH,
         )
 
-    def x2_copy(l, k):
+    def x2_copy(l, i, k):
         return pltpu.make_async_remote_copy(
-            src_ref=x2_buf.at[l, limb],
-            dst_ref=x2_buf.at[l, limb],
-            send_sem=x2_send.at[l, k - 1],
-            recv_sem=x2_recv.at[l, k - 1],
+            src_ref=x2_buf.at[l, limb, pl.ds(i * ls, ls)],
+            dst_ref=x2_buf.at[l, limb, pl.ds(i * ls, ls)],
+            send_sem=x2_send.at[l, i, k - 1],
+            recv_sem=x2_recv.at[l, i, k - 1],
             device_id={"limb": lax.rem(limb + k, nl)},
             device_id_type=MESH,
         )
@@ -364,14 +364,17 @@
     def finish_b(l, use):
         way_b = ways[l][1]
 
+        for k in range(1, nl):
+            x2_copy(l, 0, k).wait_recv()
+
         def b_part(c, carry):
             for t in range(width):
                 b_add[c * width + t] = corrected(l, 0, c * width + t)
             return carry
 
         lax.fori_loop(0, chunks, b_part, 0)
-        for c in range(chunks):
-            way_b.arrive(c, (parent_ref[l, n - 1], parent_ref[l, 0]))
+        way_b.arrive(chunks - 1, (parent_ref[l, n - 1], parent_ref[l, 0]))
+        for c in range(chunks):
             way_b.settle(c)
             for t in range(c * width, (c + 1) * width):
                 way_b.take(
@@ -438,10 +441,11 @@
         everything = pl.ds(0, 2 * ls)
         z_copy(z2_buf, z2_sem, l, 0, everything).start()
         z_copy(z2_buf, z2_sem, l, 0, everything).wait_recv()
-        for e in range(2 * ls):
-            x2_buf[l, limb, e] = mixed(z2_buf, l, e).astype(jnp.bfloat16)
-        for k in range(1, nl):
-            x2_copy(l, k).start()
+        for i in (1, 0):
+            for e in range(i * ls, (i + 1) * ls):
+                x2_buf[l, limb, e] = mixed(z2_buf, l, e).astype(jnp.bfloat16)
+            for k in range(1, nl):
+                x2_copy(l, i, k).start()
 
         def main_targets(c, carry):
             for t in range(width):
@@ -452,8 +456,10 @@
             return carry
 
         lax.fori_loop(0, chunks, main_targets, 0)
+        for c in range(chunks - 1):
+            way_b.arrive(c, needed)
         for k in range(1, nl):
-            x2_copy(l, k).wait_recv()
+            x2_copy(l, 1, k).wait_recv()
 
         last = l == levels - 1
         for c in range(chunks):
@@ -510,14 +516,14 @@
                 x_copy(l, t, k).wait_send()
         z_copy(z2_buf, z2_sem, l, 0, pl.ds(0, 2 * ls)).wait_send()
         for k in range(1, nl):
-            x2_copy(l, k).wait_send()
+            x2_copy(l, 0, k).wait_send()
+            x2_copy(l, 1, k).wait_send()
     for way in final:
         way.end()
 
 
-def deliver(n, cap, owner_ref, keys_ref, out_ref, zeros, sem):
+def deliver(n, cap, owner_ref, keys_ref, out_ref, held, load_sem, sem):
     me = lax.axis_index("leaf")
-    zeros[...] = jnp.zeros_like(zeros)
 
     def seek(j, state):
         count, sources, found = state
@@ -535,16 +541,26 @@
             @pl.when(found[s] > 0)
             def _():
                 pltpu.make_async_copy(
-                    keys_ref.at[i, sources[s]], out_ref.at[s, i], sem.at[s, i]
+                    keys_ref.at[i, sources[s]], held.at[s, i], load_sem.at[s, i]
                 ).start()
 
             @pl.when(found[s] == 0)
             def _():
-                pltpu.make_async_copy(zeros, out_ref.at[s, i], sem.at[s, i]).start()
+                held[s, i] = jnp.zeros_like(held[s, i])
 
     for s in range(cap):
         for i in range(2):
-            pltpu.make_async_copy(zeros, out_ref.at[s, i], sem.at[s, i]).wait()
+
+            @pl.when(found[s] > 0)
+            def _():
+                pltpu.make_async_copy(
+                    keys_ref.at[i, sources[s]], held.at[s, i], load_sem.at[s, i]
+                ).wait()
+
+            pltpu.make_async_copy(held.at[s, i], out_ref.at[s, i], sem.at[s, i]).start()
+    for s in range(cap):
+        for i in range(2):
+            pltpu.make_async_copy(held.at[s, i], out_ref.at[s, i], sem.at[s, i]).wait()
 
 
 def per_device(
@@ -614,8 +630,8 @@
             dma((levels, lm, nl - 1)),
             dma((levels, lm, nl - 1)),
             dma((levels, 2, 1)),
-            dma((levels, nl - 1)),
-            dma((levels, nl - 1)),
+            dma((levels, 2, nl - 1)),
+            dma((levels, 2, nl - 1)),
         ],
         compiler_params=pltpu.CompilerParams(
             collective_id=0, has_side_effects=True, vmem_limit_bytes=56 * 1024 * 1024
@@ -640,7 +656,7 @@
         out_shape=jax.ShapeDtypeStruct((cap, 2, lm) + tile, bf16),
         in_specs=[smem, hbm],
         out_specs=hbm,
-        scratch_shapes=[pltpu.VMEM((lm,) + tile, bf16), dma((cap, 2))],
+        scratch_shapes=[pltpu.VMEM((cap, 2, lm) + tile, bf16), dma((cap, 2)), dma((cap, 2))],
         compiler_params=pltpu.CompilerParams(vmem_limit_bytes=56 * 1024 * 1024),
         name="deliver",
     )(owner_table, keys)

time: 121 us -> 88.2 us (0.73)
  the two profiles are of different devices: /device:TPU:23 before, /device:TPU:0 now
where the time goes in v3:
time: 88.2 us; the launch traced here: 88 us
  Pallas kernels  88 us (100%)
    pallas_call x1, Pallas kernels, per_device(): pl.pallas_call(functools.partial(kernel, cfg), out_shape=jax.ShapeDtypeSt...  85.2 us
    pallas_call x1, Pallas kernels, per_device(): pl.pallas_call(functools.partial(deliver, n, cap), out_shape=jax.ShapeDty...  2.79 us

profile of v3, /device:TPU:0, one launch (start us, length us, event | category | flops | bytes accessed | tf_op | source)
XLA Modules:
  0.0 88.0 jit_solution(18209158468369545787)
XLA Ops:
  0.0 85.2 %derive_and_deliver.1.keys_ref = bf16[2,4,6,128,128]{4,3,2,1,0:T(8,128)(2,1)} custom-call(s32[2,4]{1,0:T(2,128)} %parent_ref.1, bf16[3,4,16]{2,1,0:T(4,128)(2,1)} %bitcast.7, bf16[4,6]{1,0:T(4,128)(2,1)} %bitcast.8, f32[6]{0:T(128)} %inv_ref.1, bf16[128,128]{1,0:T(8,128)(2,1)} %constant.10.clone.c1_ref, bf16[128,128]{1,0:T(8,128)(2,1)} %constant.11.clone.c1t_ref, ...), custom_call_target="tpu_custom_call" | custom-call | tf_op jit(solution)/shard_map/derive_and_deliver/pallas_call | solution.py:599
  85.2 2.8 %deliver.1 = bf16[3,2,6,128,128]{4,3,2,1,0:T(8,128)(2,1)} custom-call(s32[4]{0:T(128)} %owner_ref.1, bf16[2,4,6,128,128]{4,3,2,1,0:T(8,128)(2,1)} %derive_and_deliver.1.keys_ref), custom_call_target="tpu_custom_call" | custom-call | tf_op jit(solution)/shard_map/deliver/pallas_call | solution.py:654
